TPU v7x, 128 devices: a whole 4x4x4 slice. The times are simulated.
128 devices in a mesh: segment: 4 (over x), seq: 32 (over z, y, core).
Axes of the slice: x: 4, y: 4, z: 4, core: 2. Of those that a mesh axis runs over, the one named last changes fastest.
Arguments:
- token_ids: int32 [256], P('seq'), may hold values from 0 to 511
- cached_len: int32 [2], replicated, may hold values from 128 to 786432
- embed: bfloat16 [512, 8192], P(None, 'seq'), may hold values from -6 to 6
- gain: float32 [4, 8192], P('segment'), may hold values from 0.1 to 1.9
- w_in: bfloat16 [4, 8192, 3, 8192], P('segment', None, None, 'seq'), may hold values from -0.0625 to 0.0625
- short_filter: float32 [4, 7, 3, 8192], P('segment', None, None, 'seq'), may hold values from -2.5 to 2.5
- long_filter: float32 [4, 128, 512], P('segment', None, 'seq'), may hold values from -0.5 to 0.5
- w_out: bfloat16 [4, 8192, 8192], P('segment', None, 'seq'), may hold values from -0.0625 to 0.0625
- short_cycle: bfloat16 [4, 2, 128, 3, 8192], P('segment', None, None, None, 'seq'), may hold values from -6 to 6
- long_cycle: bfloat16 [4, 2, 128, 8192], P('segment', None, None, 'seq'), may hold values from -6 to 6
Outputs:
- section_out: bfloat16 [4, 256, 8192], P('segment', None, 'seq')
- new_short_cycle: bfloat16 [4, 2, 128, 3, 8192], P('segment', None, None, None, 'seq')
- new_long_cycle: bfloat16 [4, 2, 128, 8192], P('segment', None, None, 'seq')
All inputs are finite; a program needn't handle non-finite values.
Results may differ from a plain program's by a relative error of at most 0.023.
Values may be sent and summed in bfloat16 or wider, within the bound.
A program may use at most 128 MiB of HBM per device.

v0:
```python
import jax
import jax.numpy as jnp
from jax import lax
from jax.sharding import PartitionSpec as P

D = 8192
G = 512
VOCAB = 512
SHORT = 7
LONG = 128
REQUESTS = 2


def from_behind(block, axis, distance):
    devices = range(lax.axis_size(axis))
    route = [(i - distance, i) for i in devices if i - distance in devices]
    return lax.ppermute(block, axis, route)


def cycle_rows(cycle, offset):
    doubled = jnp.concatenate([cycle, cycle], axis=0)
    return lax.dynamic_slice_in_dim(doubled, offset, cycle.shape[0], 0)


def local(
    token_ids,
    cached_len,
    embed,
    gain,
    w_in,
    short_filter,
    long_filter,
    w_out,
    short_cycle,
    long_cycle,
):
    my_segment = lax.axis_index("segment")
    segments = lax.axis_size("segment")
    ids_all = lax.all_gather(token_ids, "seq", axis=0, tiled=True)
    tokens = ids_all.shape[0]
    appended = tokens // REQUESTS
    channels = embed.shape[1]
    vocab_ids = jnp.arange(VOCAB, dtype=jnp.int32)
    one_hot = (ids_all[:, None] == vocab_ids[None, :]).astype(jnp.bfloat16)
    start_rows = jnp.dot(one_hot, embed, preferred_element_type=jnp.float32).astype(jnp.bfloat16)
    gain_row = gain[0]
    proj_in = w_in[0].reshape(D, 3 * channels)
    short_taps = short_filter[0]
    kernel = jnp.repeat(long_filter[0], D // G, axis=1)[::-1][:, None, :]
    proj_out = w_out[0]
    short_cache = short_cycle[0]
    long_cache = long_cycle[0]
    every_request = list(range(REQUESTS))
    current = start_rows
    result_rows = jnp.zeros_like(start_rows)
    short_result = short_cache
    long_result = long_cache
    for turn_number in range(segments):
        number = len(every_request)
        gathered = lax.all_gather(current, "seq", axis=1, tiled=True)
        widened = gathered.astype(jnp.float32)
        scaling = lax.rsqrt(jnp.mean(widened * widened, axis=1, keepdims=True) + 1e-06)
        normed = (widened * scaling * gain_row[None, :]).astype(jnp.bfloat16)
        projected = jnp.dot(normed, proj_in, preferred_element_type=jnp.float32)
        projected = projected.astype(jnp.bfloat16).reshape(number * appended, 3, channels)
        mixed_parts = []
        short_cycles = []
        long_cycles = []
        for position, request in enumerate(every_request):
            prefix = lax.dynamic_index_in_dim(cached_len, request, 0, keepdims=False)
            own_rows = projected[position * appended : (position + 1) * appended]
            short_old = lax.dynamic_index_in_dim(short_cache, request, 0, keepdims=False)
            long_old = lax.dynamic_index_in_dim(long_cache, request, 0, keepdims=False)
            extended = jnp.concatenate([cycle_rows(short_old, prefix % LONG), own_rows], axis=0)
            wide_ext = extended.astype(jnp.float32)
            filtered = jnp.zeros((appended, 3, channels), jnp.float32)
            for tap_index in range(SHORT):
                filtered = (
                    filtered
                    + short_taps[tap_index][None]
                    * wide_ext[LONG - tap_index : LONG - tap_index + appended]
                )
            product = (filtered[:, 1] * filtered[:, 2]).astype(jnp.bfloat16)
            carried = jnp.concatenate([cycle_rows(long_old, prefix % LONG), product], axis=0)
            convolved = lax.conv_general_dilated(
                carried[1:].astype(jnp.float32)[None],
                kernel,
                window_strides=(1,),
                padding="VALID",
                dimension_numbers=("NWC", "WIO", "NWC"),
                feature_group_count=channels,
                precision=lax.Precision.HIGHEST,
            )[0]
            mixed_parts.append((filtered[:, 0] * convolved).astype(jnp.bfloat16))
            backward = (LONG - (prefix + appended) % LONG) % LONG
            short_cycles.append(cycle_rows(extended[appended:], backward))
            long_cycles.append(cycle_rows(carried[appended:], backward))
        mixed = jnp.concatenate(mixed_parts, axis=0)
        initial = jnp.zeros((number * appended, channels), jnp.float32)
        shard_piece = lax.all_gather(mixed, "seq", axis=1, tiled=True)
        weight_rows = lax.slice_in_dim(proj_out, 0, shard_piece.shape[1], axis=0)
        summed = initial + jnp.dot(shard_piece, weight_rows, preferred_element_type=jnp.float32)
        output_rows = (current.astype(jnp.float32) + summed).astype(jnp.bfloat16)
        output_rows, short_cycles, long_cycles = (output_rows, short_cycles, long_cycles)
        is_mine = my_segment == turn_number
        result_rows = jnp.where(is_mine, output_rows, result_rows)
        short_result = jnp.where(is_mine, jnp.stack(short_cycles), short_result)
        long_result = jnp.where(is_mine, jnp.stack(long_cycles), long_result)
        if turn_number + 1 < segments:
            received = from_behind(output_rows, "segment", 1)
            current = jnp.where(my_segment == 0, start_rows, received)
    return (result_rows[None], short_result[None], long_result[None])


def solution(mesh):
    in_specs = (
        P("seq"),
        P(),
        P(None, "seq"),
        P("segment", None),
        P("segment", None, None, "seq"),
        P("segment", None, None, "seq"),
        P("segment", None, "seq"),
        P("segment", None, "seq"),
        P("segment", None, None, None, "seq"),
        P("segment", None, None, "seq"),
    )
    out_specs = (
        P("segment", None, "seq"),
        P("segment", None, None, None, "seq"),
        P("segment", None, None, "seq"),
    )
    return jax.shard_map(local, mesh=mesh, in_specs=in_specs, out_specs=out_specs, check_vma=False)
```

profile of v0, /device:TPU:7, one launch (start us, length us, event | category | flops | bytes accessed | tf_op | source)
XLA Modules:
  0.0 537.6 jit_solution(9733577705821494347)
XLA Ops:
  7.2 1.3 dynamic-slice.4
  9.2 0.9 dynamic-update-slice
  10.0 14.9 %all-reduce = s32[256]{0:T(256)S(1)} all-reduce(s32[256]{0:T(256)S(1)} %dynamic-update-slice), channel_id=1, replica_groups=mesh['segment'=4,'seq'=32] {'seq'}, use_global_device_ids=true, to_apply=%add | all-reduce | flops 256 | bytes 2048
  24.9 0.9 convolution_convert_fusion
  25.9 1.4 fusion.202
  31.3 16.7 %copy.58 = bf16[1,8192,3,256]{1,3,2,0:T(8,128)(2,1)} copy(bf16[1,8192,3,256]{3,1,2,0:T(8,128)(2,1)} %param.14) | data formatting | bytes 25165824 | tf_op args[4]
  49.4 26.1 %all-gather.9.cloned.1.call-done = bf16[256,8192]{1,0:T(8,128)(2,1)} async-done(((bf16[256,256]{1,0:T(8,128)(2,1)}), bf16[256,8192]{1,0:T(8,128)(2,1)}) %all-gather.9.cloned.1.call-update) | async-done | bytes 4194320 | tf_op jit(solution)/shard_map/all_gather | solution.py:60
  75.5 3.3 fusion
  78.9 8.2 %fusion.36 = bf16[256,768]{1,0:T(8,128)(2,1)S(1)} fusion(bf16[8192,768]{0,1:T(8,128)(2,1)} %bitcast.197, bf16[256,8192]{1,0:T(8,128)(2,1)S(1)} %copy-done.2, f32[8192]{0:T(1024)S(1)} %bitcast.236, f32[256]{0:T(256)S(1)} %add_rsqrt_fusion.3), kind=kOutput, calls=%fused_computation.40 | convolution fusion | flops 3229810688 | bytes 17204224 | tf_op jit(solution)/shard_map/dot_general | solution.py:64
  88.0 1.4 fusion.125
  90.2 1.4 fusion.123
  91.7 0.7 pad_maximum_fusion.16
  92.4 48.9 %all-gather.11.cloned.1.call-done = bf16[256,8192]{1,0:T(8,128)(2,1)} async-done(((bf16[256,256]{1,0:T(8,128)(2,1)}), bf16[256,8192]{1,0:T(8,128)(2,1)}) %all-gather.11.cloned.1.call-update) | async-done | bytes 4194320 | tf_op jit(solution)/shard_map/all_gather | solution.py:100
  141.3 4.7 fusion.51
  146.0 1.3 collective-permute-start
  147.4 5.4 %collective-permute-done = bf16[256,256]{1,0:T(8,128)(2,1)S(1)} collective-permute-done((bf16[256,256]{1,0:T(8,128)(2,1)S(1)}, bf16[256,256]{1,0:T(8,128)(2,1)S(1)}, u32[]{:S(2)}, u32[]{:S(2)}) %collective-permute-start) | collective-permute-done | bytes 131104 | tf_op jit(solution)/shard_map/ppermute | solution.py:17
  152.8 0.7 broadcast_select_fusion.2
  153.8 49.4 %all-gather.13.cloned.1.call-done = bf16[256,8192]{1,0:T(8,128)(2,1)} async-done(((bf16[256,256]{1,0:T(8,128)(2,1)}), bf16[256,8192]{1,0:T(8,128)(2,1)}) %all-gather.13.cloned.1.call-update) | async-done | bytes 4194320 | tf_op jit(solution)/shard_map/all_gather | solution.py:60
  203.3 3.3 fusion.3
  206.7 8.2 %fusion.39 = bf16[256,768]{1,0:T(8,128)(2,1)S(1)} fusion(bf16[8192,768]{0,1:T(8,128)(2,1)} %bitcast.198, bf16[256,8192]{1,0:T(8,128)(2,1)S(1)} %copy-done.4, f32[256]{0:T(256)S(1)} %add_rsqrt_fusion.2, f32[8192]{0:T(1024)S(1)} %bitcast.237), kind=kOutput, calls=%fused_computation.41 | convolution fusion | flops 3229810688 | bytes 17204224 | tf_op jit(solution)/shard_map/dot_general | solution.py:64
  215.8 1.4 fusion.121
  218.0 1.4 fusion.119
  219.5 0.7 pad_maximum_fusion.17
  220.2 48.9 %all-gather.15.cloned.1.call-done = bf16[256,8192]{1,0:T(8,128)(2,1)} async-done(((bf16[256,256]{1,0:T(8,128)(2,1)}), bf16[256,8192]{1,0:T(8,128)(2,1)}) %all-gather.15.cloned.1.call-update) | async-done | bytes 4194320 | tf_op jit(solution)/shard_map/all_gather | solution.py:100
  269.1 4.7 add_convert_fusion.2
  273.9 1.3 collective-permute-start.1
  275.2 5.4 %collective-permute-done.1 = bf16[256,256]{1,0:T(8,128)(2,1)S(1)} collective-permute-done((bf16[256,256]{1,0:T(8,128)(2,1)S(1)}, bf16[256,256]{1,0:T(8,128)(2,1)S(1)}, u32[]{:S(2)}, u32[]{:S(2)}) %collective-permute-start.1) | collective-permute-done | bytes 131104 | tf_op jit(solution)/shard_map/ppermute | solution.py:17
  280.6 0.7 broadcast_select_fusion.1
  281.9 49.2 %all-gather.17.cloned.1.call-done = bf16[256,8192]{1,0:T(8,128)(2,1)} async-done(((bf16[256,256]{1,0:T(8,128)(2,1)}), bf16[256,8192]{1,0:T(8,128)(2,1)}) %all-gather.17.cloned.1.call-update) | async-done | bytes 4194320 | tf_op jit(solution)/shard_map/all_gather | solution.py:60
  331.1 3.3 fusion.6
  334.5 8.2 %fusion.42 = bf16[256,768]{1,0:T(8,128)(2,1)S(1)} fusion(bf16[8192,768]{0,1:T(8,128)(2,1)} %bitcast.199, bf16[256,8192]{1,0:T(8,128)(2,1)S(1)} %copy-done.5, f32[256]{0:T(256)S(1)} %add_rsqrt_fusion.1, f32[8192]{0:T(1024)S(1)} %bitcast.238), kind=kOutput, calls=%fused_computation.42 | convolution fusion | flops 3229810688 | bytes 17204224 | tf_op jit(solution)/shard_map/dot_general | solution.py:64
  343.6 1.4 fusion.117
  346.0 1.4 fusion.115
  348.1 48.9 %all-gather.19.cloned.1.call-done = bf16[256,8192]{1,0:T(8,128)(2,1)} async-done(((bf16[256,256]{1,0:T(8,128)(2,1)}), bf16[256,8192]{1,0:T(8,128)(2,1)}) %all-gather.19.cloned.1.call-update) | async-done | bytes 4194320 | tf_op jit(solution)/shard_map/all_gather | solution.py:100
  397.0 4.7 add_convert_fusion.1
  401.8 1.3 collective-permute-start.2
  403.1 5.4 %collective-permute-done.2 = bf16[256,256]{1,0:T(8,128)(2,1)S(1)} collective-permute-done((bf16[256,256]{1,0:T(8,128)(2,1)S(1)}, bf16[256,256]{1,0:T(8,128)(2,1)S(1)}, u32[]{:S(2)}, u32[]{:S(2)}) %collective-permute-start.2) | collective-permute-done | bytes 131104 | tf_op jit(solution)/shard_map/ppermute | solution.py:17
  408.5 0.7 broadcast_select_fusion
  409.4 49.6 %all-gather.21.cloned.1.call-done = bf16[256,8192]{1,0:T(8,128)(2,1)} async-done(((bf16[256,256]{1,0:T(8,128)(2,1)}), bf16[256,8192]{1,0:T(8,128)(2,1)}) %all-gather.21.cloned.1.call-update) | async-done | bytes 4194320 | tf_op jit(solution)/shard_map/all_gather | solution.py:60
  459.0 3.3 fusion.9
  462.4 8.2 %fusion.45 = bf16[256,768]{1,0:T(8,128)(2,1)S(1)} fusion(bf16[8192,768]{0,1:T(8,128)(2,1)} %bitcast.200, bf16[256,8192]{1,0:T(8,128)(2,1)S(1)} %copy-done.3, f32[256]{0:T(256)S(1)} %add_rsqrt_fusion, f32[8192]{0:T(1024)S(1)} %bitcast.239), kind=kOutput, calls=%fused_computation.43 | convolution fusion | flops 3229810688 | bytes 17204224 | tf_op jit(solution)/shard_map/dot_general | solution.py:64
  472.3 1.6 fusion.113
  474.0 1.4 fusion.111
  475.4 0.7 pad_maximum_fusion.19
  481.7 0.7 maximum_select_fusion.4
  482.4 0.9 maximum_select_fusion
  483.3 41.8 %all-gather.23.cloned.1.call-done = bf16[256,8192]{1,0:T(8,128)(2,1)} async-done(((bf16[256,256]{1,0:T(8,128)(2,1)}), bf16[256,8192]{1,0:T(8,128)(2,1)}) %all-gather.23.cloned.1.call-update) | async-done | bytes 4194320 | tf_op jit(solution)/shard_map/all_gather | solution.py:100
  525.1 5.4 %fusion.146 = bf16[1,256,256]{2,1,0:T(8,128)(2,1)} fusion(bf16[256,256]{1,0:T(8,128)(2,1)S(1)} %copy-done.8, bf16[256,256]{1,0:T(8,128)(2,1)} %copy-done.23, bf16[256,256]{1,0:T(8,128)(2,1)S(1)} %copy-done.22, bf16[256,256]{1,0:T(8,128)(2,1)S(1)} %copy-done.20, pred[]{:T(512)S(6)} %eq.67, pred[]{:T(512)S(6)} %eq.66, pred[]{:T(512)S(6)} %eq.62, ...), kind=kOutput, calls=%fused_computation.241 | convolution fusion | flops 1074200576 | bytes 9043972 | tf_op jit(solution)/shard_map/dot_general | solution.py:102
  (168 shorter events, 14.6 us)
Async XLA Ops:
  7.2 17.8 %copy-start = (bf16[512,256]{1,0:T(8,128)(2,1)S(1)}, bf16[512,256]{1,0:T(8,128)(2,1)}, u32[]{:S(2)}) copy-start(bf16[512,256]{1,0:T(8,128)(2,1)} %param.12) | copy-start | bytes 786436
  7.2 68.3 %all-gather.9.cloned.1.call-start = ((), (), s32[]{:S(2)}) async-start(), calls=%async_computation | async-start | bytes 4325376 | tf_op jit(solution)/shard_map/all_gather | solution.py:60
  25.9 115.4 %all-gather.11.cloned.1.call-start = ((), (), s32[]{:S(2)}) async-start(), calls=%async_computation.1 | async-start | bytes 4325376 | tf_op jit(solution)/shard_map/all_gather | solution.py:100
  31.3 16.8 %copy-start.17 = (f32[1,7,3,256]{3,0,2,1:T(1,128)S(1)}, f32[1,7,3,256]{3,0,2,1:T(1,128)}, u32[]{:S(2)}) copy-start(f32[1,7,3,256]{3,0,2,1:T(1,128)} %param.15) | copy-start | bytes 64516
  31.3 16.8 %copy-start.18 = (f32[1,128,16]{1,2,0:T(8,128)S(1)}, f32[1,128,16]{1,2,0:T(8,128)}, u32[]{:S(2)}) copy-start(f32[1,128,16]{1,2,0:T(8,128)} %param.16) | copy-start | bytes 24580
  31.3 17.2 %copy-start.11 = (bf16[1,2,128,256]{3,2,1,0:T(8,128)(2,1)S(1)}, bf16[1,2,128,256]{3,2,1,0:T(8,128)(2,1)}, u32[]{:S(2)}) copy-start(bf16[1,2,128,256]{3,2,1,0:T(8,128)(2,1)} %param.19) | copy-start | bytes 393220
  31.3 17.5 %copy-start.7 = (bf16[1,2,128,3,256]{4,2,3,1,0:T(8,128)(2,1)S(1)}, bf16[1,2,128,3,256]{4,2,3,1,0:T(8,128)(2,1)}, u32[]{:S(2)}) copy-start(bf16[1,2,128,3,256]{4,2,3,1,0:T(8,128)(2,1)} %param.18) | copy-start | bytes 1179652
  48.0 30.7 %copy-start.24 = (f32[1,8192]{1,0:T(1,128)S(1)}, f32[1,8192]{1,0:T(1,128)}, u32[]{:S(2)}) copy-start(f32[1,8192]{1,0:T(1,128)} %param.13) | copy-start | bytes 98308
  48.4 295.2 %copy-start.13 = (f32[128,1,256]{2,1,0:T(1,128)}, f32[128,1,256]{2,1,0:T(1,128)S(1)}, u32[]{:S(2)}) copy-start(f32[128,1,256]{2,1,0:T(1,128)S(1)} %copy.62) | copy-start | bytes 393220
  75.4 3.4 copy-start.2
  90.2 51.1 %copy-start.6 = (bf16[256,256]{1,0:T(8,128)(2,1)S(1)}, bf16[256,256]{1,0:T(8,128)(2,1)}, u32[]{:S(2)}) copy-start(bf16[256,256]{1,0:T(8,128)(2,1)} %convolution_convert_fusion) | copy-start | bytes 393220
  92.4 110.9 %all-gather.13.cloned.1.call-start = ((), (), s32[]{:S(2)}) async-start(), calls=%async_computation.2 | async-start | bytes 4325376 | tf_op jit(solution)/shard_map/all_gather | solution.py:60
  146.0 68.9 %copy-start.19 = (bf16[256,256]{1,0:T(8,128)(2,1)}, bf16[256,256]{1,0:T(8,128)(2,1)S(1)}, u32[]{:S(2)}) copy-start(bf16[256,256]{1,0:T(8,128)(2,1)S(1)} %fusion.51) | copy-start | bytes 393220
  146.0 6.7 %collective-permute-start = (bf16[256,256]{1,0:T(8,128)(2,1)S(1)}, bf16[256,256]{1,0:T(8,128)(2,1)S(1)}, u32[]{:S(2)}, u32[]{:S(2)}) collective-permute-start(bf16[256,256]{1,0:T(8,128)(2,1)S(1)} %fusion.51), channel_id=1, source_target_pairs={{0,32},{32,64},{64,96},{1,33},{33,65},{65,97},{2,34},{34,66},{66,9... | collective-permute-start | bytes 393224 | tf_op jit(solution)/shard_map/ppermute | solution.py:17
  153.5 115.7 %all-gather.15.cloned.1.call-start = ((), (), s32[]{:S(2)}) async-start(), calls=%async_computation.3 | async-start | bytes 4325376 | tf_op jit(solution)/shard_map/all_gather | solution.py:100
  203.3 3.4 copy-start.4
  218.0 51.1 %copy-start.9 = (bf16[256,256]{1,0:T(8,128)(2,1)S(1)}, bf16[256,256]{1,0:T(8,128)(2,1)}, u32[]{:S(2)}) copy-start(bf16[256,256]{1,0:T(8,128)(2,1)} %broadcast_select_fusion.2) | copy-start | bytes 393220
  220.2 110.9 %all-gather.17.cloned.1.call-start = ((), (), s32[]{:S(2)}) async-start(), calls=%async_computation.4 | async-start | bytes 4325376 | tf_op jit(solution)/shard_map/all_gather | solution.py:60
  273.9 68.9 %copy-start.21 = (bf16[256,256]{1,0:T(8,128)(2,1)}, bf16[256,256]{1,0:T(8,128)(2,1)S(1)}, u32[]{:S(2)}) copy-start(bf16[256,256]{1,0:T(8,128)(2,1)S(1)} %add_convert_fusion.2) | copy-start | bytes 393220
  273.9 6.7 %collective-permute-start.1 = (bf16[256,256]{1,0:T(8,128)(2,1)S(1)}, bf16[256,256]{1,0:T(8,128)(2,1)S(1)}, u32[]{:S(2)}, u32[]{:S(2)}) collective-permute-start(bf16[256,256]{1,0:T(8,128)(2,1)S(1)} %add_convert_fusion.2), channel_id=1, source_target_pairs={{0,32},{32,64},{64,96},{1,33},{33,65},{65,97},{2,34},{34,66},{66,9... | collective-permute-start | bytes 393224 | tf_op jit(solution)/shard_map/ppermute | solution.py:17
  281.3 115.7 %all-gather.19.cloned.1.call-start = ((), (), s32[]{:S(2)}) async-start(), calls=%async_computation.5 | async-start | bytes 4325376 | tf_op jit(solution)/shard_map/all_gather | solution.py:100
  331.1 3.4 copy-start.5
  345.1 0.9 copy-start.14
  346.0 51.1 %copy-start.10 = (bf16[256,256]{1,0:T(8,128)(2,1)S(1)}, bf16[256,256]{1,0:T(8,128)(2,1)}, u32[]{:S(2)}) copy-start(bf16[256,256]{1,0:T(8,128)(2,1)} %broadcast_select_fusion.1) | copy-start | bytes 393220
  348.1 110.9 %all-gather.21.cloned.1.call-start = ((), (), s32[]{:S(2)}) async-start(), calls=%async_computation.6 | async-start | bytes 4325376 | tf_op jit(solution)/shard_map/all_gather | solution.py:60
  401.8 60.5 %copy-start.23 = (bf16[256,256]{1,0:T(8,128)(2,1)}, bf16[256,256]{1,0:T(8,128)(2,1)S(1)}, u32[]{:S(2)}) copy-start(bf16[256,256]{1,0:T(8,128)(2,1)S(1)} %add_convert_fusion.1) | copy-start | bytes 393220
  401.8 6.7 %collective-permute-start.2 = (bf16[256,256]{1,0:T(8,128)(2,1)S(1)}, bf16[256,256]{1,0:T(8,128)(2,1)S(1)}, u32[]{:S(2)}, u32[]{:S(2)}) collective-permute-start(bf16[256,256]{1,0:T(8,128)(2,1)S(1)} %add_convert_fusion.1), channel_id=1, source_target_pairs={{0,32},{32,64},{64,96},{1,33},{33,65},{65,97},{2,34},{34,66},{66,9... | collective-permute-start | bytes 393224 | tf_op jit(solution)/shard_map/ppermute | solution.py:17
  409.2 115.9 %all-gather.23.cloned.1.call-start = ((), (), s32[]{:S(2)}) async-start(), calls=%async_computation.7 | async-start | bytes 4325376 | tf_op jit(solution)/shard_map/all_gather | solution.py:100
  459.0 3.4 copy-start.3
  471.1 1.2 copy-start.15
  472.3 1.7 copy-start.16
  475.4 6.3 %copy-start.12 = (bf16[1,2,128,256]{3,2,1,0:T(8,128)(2,1)S(1)}, bf16[1,2,128,256]{3,2,1,0:T(8,128)(2,1)}, u32[]{:S(2)}) copy-start(bf16[1,2,128,256]{3,2,1,0:T(8,128)(2,1)} %param.19) | copy-start | bytes 393220
  478.8 46.4 %copy-start.8 = (bf16[256,256]{1,0:T(8,128)(2,1)S(1)}, bf16[256,256]{1,0:T(8,128)(2,1)}, u32[]{:S(2)}) copy-start(bf16[256,256]{1,0:T(8,128)(2,1)} %broadcast_select_fusion) | copy-start | bytes 393220
  478.8 46.3 %copy-start.20 = (bf16[256,256]{1,0:T(8,128)(2,1)S(1)}, bf16[256,256]{1,0:T(8,128)(2,1)}, u32[]{:S(2)}) copy-start(bf16[256,256]{1,0:T(8,128)(2,1)} %copy-done.19) | copy-start | bytes 393220
  478.8 46.3 %copy-start.22 = (bf16[256,256]{1,0:T(8,128)(2,1)S(1)}, bf16[256,256]{1,0:T(8,128)(2,1)}, u32[]{:S(2)}) copy-start(bf16[256,256]{1,0:T(8,128)(2,1)} %copy-done.21) | copy-start | bytes 393220
  525.1 5.4 %copy-start.1 = (bf16[512,256]{1,0:T(8,128)(2,1)S(1)}, bf16[512,256]{1,0:T(8,128)(2,1)}, u32[]{:S(2)}) copy-start(bf16[512,256]{1,0:T(8,128)(2,1)} %param.12) | copy-start | bytes 786436
Sparse Core Ops, SparseCore 0:
  26.0 49.3 all-gather.8
  92.5 48.7 all-gather.10
  153.6 49.6 all-gather.12
  220.3 48.7 all-gather.14
  281.4 49.6 all-gather.16
  348.2 48.7 all-gather.18
  409.3 49.6 all-gather.20
  476.3 48.7 all-gather.22
where the time goes:
time: 547 us; the launch traced here: 538 us
  waiting for transfers between devices  379 us (69%)
  matrix products  64.9 us (12%)
  other arithmetic  26.7 us (5%)
  local copies, waits for them, and re-layouts  25.4 us (5%)
  between operations  21.3 us (4%)
  blocking collectives  14.9 us (3%)
    all_gather x4, waiting for transfers between devices, local(): shard_piece = lax.all_gather(mixed, 'seq', axis=1, tiled=True)  189 us
    all_gather x4, waiting for transfers between devices, local(): gathered = lax.all_gather(current, 'seq', axis=1, tiled=True)  174 us
    dot_general x4, matrix products, local(): projected = jnp.dot(normed, proj_in, preferred_element_type=jnp.float32)  33 us
    unnamed x58, local copies, waits for them, and re-layouts  19.8 us
    dot_general x4, matrix products, local(): jnp.dot(shard_piece, weight_rows, preferred_element_type=jnp.float32)  19.5 us
    ppermute x3, waiting for transfers between devices, from_behind(): return lax.ppermute(block, axis, route)  16.3 us
    unnamed x1, blocking collectives  14.9 us
    reduce_sum x4, other arithmetic, local(): jnp.mean(widened * widened, axis=1, keepdims=True) + 1e-06  13 us
  transfers between devices with their start and end apart: 11, of which 11 were waited for; matrix products, arithmetic and copies ran while one was open for 5% of the time, Pallas kernels for 0%

commit v1 on v0

v1 whole, which is shorter than its diff:
```python
import jax
import jax.numpy as jnp
from jax import lax
from jax.experimental import pallas as pl
from jax.experimental.pallas import tpu as pltpu
from jax.sharding import PartitionSpec as P

D = 8192
SHORT = 7
LONG = 128
REQUESTS = 2
SIDE = 4
CHIPS = SIDE * SIDE
ROWS = 64
CHUNKS = 4
BLOCK = 256
WIDE = 2 * BLOCK
GROUP = 16
GROUPS = BLOCK // GROUP
TAIL = REQUESTS * LONG
TAPS = TAIL + REQUESTS * 3 * 8
PACK = TAPS + 3 * 8
LEAD = 2
MESH = pl.DeviceIdType.MESH
F32 = jnp.float32
BF16 = jnp.bfloat16


def dot(a, b):
    return jnp.dot(a, b, preferred_element_type=F32)


def folded(i):
    return i + (i // 2) * (5 - 2 * i)


def kernel(
    ids_ref,
    len_ref,
    embed_ref,
    gain_ref,
    w_in_ref,
    short_ref,
    long_ref,
    w_out_ref,
    short_cycle_ref,
    long_cycle_ref,
    section_ref,
    new_short_ref,
    new_long_ref,
    w_in,
    w_out,
    gathered,
    section_in,
    outgoing,
    acc,
    squares,
    extended,
    masked,
    toeplitz,
    toeplitz_old,
    pack,
    reversed_taps,
    keep,
    stage,
    ids_all,
    ids_own,
    embed_other,
    section_half,
    gather_send,
    gather_recv,
    hop_send,
    hop_recv,
    w_in_send,
    w_in_recv,
    w_out_send,
    w_out_recv,
    prep_send,
    prep_recv,
    keep_send,
    keep_recv,
    half_send,
    half_recv,
    ids_send,
    ids_recv,
):
    segment = lax.axis_index("segment")
    seq = lax.axis_index("seq")
    core = lax.rem(seq, 2)
    chip = seq // 2
    row_z, row_y = chip // SIDE, lax.rem(chip, SIDE)
    sibling = (segment, chip * 2 + 1 - core)

    def chip_at(k, sign):
        dz, dy = folded(k // SIDE), folded(lax.rem(k, SIDE))
        z = lax.rem(row_z + sign * dz + SIDE, SIDE)
        y = lax.rem(row_y + sign * dy + SIDE, SIDE)
        return z * SIDE + y

    def remote(src, dst, send, recv, where):
        return pltpu.make_async_remote_copy(
            src_ref=src, dst_ref=dst, send_sem=send, recv_sem=recv, device_id=where, device_id_type=MESH
        )

    def rows_of(j):
        return pl.ds(pl.multiple_of(j * WIDE, WIDE), WIDE)

    barrier = pltpu.get_barrier_semaphore()

    def greet(k, carry):
        pl.semaphore_signal(
            barrier, inc=1, device_id=(segment, k * 2 + 1 - core), device_id_type=MESH
        )
        return carry

    lax.fori_loop(0, CHIPS, greet, 0)

    @pl.when(core == 1)
    def _():
        for step in (1, 3):
            pl.semaphore_signal(
                barrier, inc=1, device_id=(lax.rem(segment + step, 4), seq), device_id_type=MESH
            )

    def w_in_local(k):
        rows = rows_of(chip_at(k, 1))
        return pltpu.make_async_copy(
            w_in_ref.at[:, rows, :], w_in.at[0, :, rows, :], w_in_recv.at[0, k]
        )

    def w_in_remote(k):
        rows = rows_of(chip_at(k, 1))
        return remote(
            w_in_ref.at[:, rows, :], w_in.at[1, :, rows, :], w_in_send.at[k], w_in_recv.at[1, k], sibling
        )

    w_out_local = pltpu.make_async_copy(w_out_ref, w_out.at[1], w_out_recv.at[1])
    w_out_remote = remote(w_out_ref, w_out.at[0], w_out_send, w_out_recv.at[0], sibling)

    def order(i):
        return lax.rem(i + 1, CHIPS)

    @pl.when(core == 0)
    def _():
        def begin(i, carry):
            w_in_local(order(i)).start()
            return carry

        lax.fori_loop(0, CHIPS, begin, 0)

    @pl.when(core == 1)
    def _():
        w_out_local.start()

    sub = lax.broadcasted_iota(jnp.int32, (8, 128), 0)
    mine = jnp.zeros((8, 128), jnp.int32)
    for i in range(8):
        mine = jnp.where(sub == i, ids_ref[i], mine)

    @pl.when(core == 0)
    def _():
        ids_own[0:8, :] = mine

    @pl.when(core == 1)
    def _():
        ids_own[8:16, :] = mine

    @pl.when(core == 0)
    def _():
        pl.semaphore_wait(barrier, CHIPS)

    @pl.when(core == 1)
    def _():
        pl.semaphore_wait(barrier, CHIPS + 2)

    ids_pair = remote(
        ids_own.at[pl.ds(8, 8)], ids_own.at[pl.ds(8, 8)], ids_send.at[CHIPS], ids_recv.at[CHIPS], sibling
    )
    embed_half = remote(embed_ref, embed_other, prep_send.at[2], prep_recv.at[2], sibling)

    def ids_to(k):
        return remote(
            ids_own, ids_all.at[chip], ids_send.at[k], ids_recv.at[chip], (segment, k * 2 + 1)
        )

    def ids_from(k):
        return remote(ids_own, ids_all.at[k], ids_send.at[k], ids_recv.at[k], sibling)

    @pl.when((segment == 0) & (core == 1))
    def _():
        ids_pair.start()

    @pl.when((segment == 0) & (core == 0))
    def _():
        ids_pair.wait_recv()

        def give(k, carry):
            ids_to(k).start()
            return carry

        lax.fori_loop(0, CHIPS, give, 0)
        embed_half.start()

    @pl.when(core == 1)
    def _():
        def begin(i, carry):
            w_in_remote(order(i)).start()
            return carry

        lax.fori_loop(0, CHIPS, begin, 0)

    @pl.when(core == 0)
    def _():
        w_out_remote.start()

    flip_from = lax.broadcasted_iota(jnp.int32, (LONG, 2 * LONG), 0)
    flip_to = lax.broadcasted_iota(jnp.int32, (LONG, 2 * LONG), 1)
    flip = (flip_from + flip_to == LONG).astype(F32).astype(BF16)
    reversed_taps[...] = dot(long_ref[...].astype(BF16), flip)
    lane_group = lax.broadcasted_iota(jnp.int32, (1, BLOCK), 1) // GROUP

    def group_columns(g):
        return pl.ds(pl.multiple_of(g * LONG, LONG), LONG)

    def expand(g, carry):
        line = jnp.broadcast_to(reversed_taps[pl.ds(g, 1), :], (LONG, 2 * LONG))
        turned = pltpu.roll(line, 0, 1, stride=1, stride_axis=0)
        toeplitz_old[:, group_columns(g)] = turned[:, :LONG].astype(BF16)
        toeplitz[core, :, group_columns(g)] = turned[:, LONG:].astype(BF16)
        return carry

    lax.fori_loop(0, GROUPS, expand, 0)

    at_row = lax.broadcasted_iota(jnp.int32, (LONG, LONG), 0)
    at_col = lax.broadcasted_iota(jnp.int32, (LONG, LONG), 1)
    last_row = lax.broadcasted_iota(jnp.int32, (8, LONG), 0)
    last_col = lax.broadcasted_iota(jnp.int32, (8, LONG), 1)
    for r in range(REQUESTS):
        prefix = len_ref[r]
        slot = ((at_row + prefix) & (LONG - 1)) == at_col
        old = dot(slot.astype(F32).astype(BF16), long_cycle_ref[r])

        def spread(g, carry):
            masked[0, group_columns(g), :] = jnp.where(lane_group == g, old, 0.0).astype(BF16)
            return carry

        lax.fori_loop(0, GROUPS, spread, 0)
        pack[core, r * LONG : (r + 1) * LONG, :] = dot(toeplitz_old[...], masked[0])
        slot = ((last_row + (prefix - 8)) & (LONG - 1)) == last_col
        pick = slot.astype(F32).astype(BF16)
        for b in range(3):
            at = TAIL + (r * 3 + b) * 8
            pack[core, at : at + 8, :] = dot(pick, short_cycle_ref[r, b])
    for b in range(3):
        for j in range(SHORT):
            at = TAPS + b * 8 + j
            pack[core, at : at + 1, :] = short_ref[j * 3 + b]
        pack[core, TAPS + b * 8 + 7 : TAPS + b * 8 + 8, :] = jnp.zeros((1, BLOCK), F32)

    pack_copy = remote(pack.at[1], pack.at[1], prep_send.at[0], prep_recv.at[0], sibling)
    toeplitz_copy = remote(toeplitz.at[1], toeplitz.at[1], prep_send.at[1], prep_recv.at[1], sibling)

    @pl.when(core == 1)
    def _():
        pack_copy.start()
        toeplitz_copy.start()

    def spread_out(src, m):
        def begin(i, carry):
            k = order(i)
            target = (segment, chip_at(k, -1) * 2 + 1 - core)
            remote(
                src, gathered.at[m, chip], gather_send.at[m, k], gather_recv.at[m, k], target
            ).start()
            return carry

        lax.fori_loop(0, CHIPS, begin, 0)

    def arrived(m, k):
        j = chip_at(k, 1)
        remote(
            section_in.at[0], gathered.at[m, j], gather_send.at[m, k], gather_recv.at[m, k], sibling
        ).wait_recv()
        return j

    def keep_copy(m):
        return remote(stage.at[m], keep.at[m], keep_send.at[m], keep_recv.at[m], sibling)

    def half_copy(m):
        return remote(
            outgoing.at[m, :, pl.ds(0, BLOCK)], section_half.at[m], half_send.at[m], half_recv.at[m], sibling
        )

    def hop_copy(m):
        return remote(
            outgoing.at[m],
            section_in.at[m],
            hop_send.at[m],
            hop_recv.at[m],
            (lax.rem(segment + 1, 4), seq),
        )

    def write_cycles():
        for r in range(REQUESTS):
            prefix = len_ref[r]
            turn = (((at_row - prefix) & (LONG - 1)) == at_col).astype(F32).astype(BF16)
            for b in range(4):
                rows = jnp.concatenate([keep[2 * r, b], keep[2 * r + 1, b]], axis=0)
                rolled = dot(turn, rows).astype(BF16)
                if b < 3:
                    new_short_ref[r, b] = rolled
                else:
                    new_long_ref[r] = rolled

    def project(m, carry):
        acc[...] = jnp.zeros_like(acc)
        squares[...] = jnp.zeros_like(squares)

        def pair(i, inner):
            for p in range(2):
                k = order(2 * i + p)
                j = arrived(m, k)

                @pl.when(m == 0)
                def _():
                    w_in_local(k).wait()
                    w_in_remote(k).wait_recv()

                wide = gathered[m, j].astype(F32)
                power = wide * wide
                squares[...] += (
                    power[:, 0:128] + power[:, 128:256] + power[:, 256:384] + power[:, 384:512]
                )
                scaled = (wide * gain_ref[:, rows_of(j)]).astype(BF16)
                for c in range(2):
                    for b in range(3):
                        acc[c * 3 + b] += dot(scaled, w_in[c, b, rows_of(j), :])
            return inner

        lax.fori_loop(0, CHIPS // 2, pair, 0)
        scale = lax.rsqrt(jnp.sum(squares[...], axis=1, keepdims=True) * (1.0 / D) + 1e-6)
        half = lax.rem(m, 2)
        request = m // 2

        @pl.when(m == 0)
        def _():
            pack_copy.wait_recv()
            toeplitz_copy.wait_recv()

        for c in range(2):
            filtered = []
            for b in range(3):
                e = c * 3 + b
                own = (acc[e] * scale).astype(BF16)
                if c == 0:
                    keep[m, b] = own
                else:
                    stage[m, b] = own

                @pl.when(half == 0)
                def _():
                    at = pl.multiple_of(TAIL + (request * 3 + b) * 8, 8)
                    extended[e, 0:8, :] = pack[c, pl.ds(at, 8), :]

                @pl.when(half == 1)
                def _():
                    extended[e, 0:8, :] = extended[e, ROWS : ROWS + 8, :]

                extended[e, 8 : 8 + ROWS, :] = own.astype(F32)
                total = jnp.zeros((ROWS, BLOCK), F32)
                for j in range(SHORT):
                    at = TAPS + b * 8 + j
                    total = total + pack[c, at : at + 1, :] * extended[e, 8 - j : 8 - j + ROWS, :]
                filtered.append(total)
            product = (filtered[1] * filtered[2]).astype(BF16)
            if c == 0:
                keep[m, 3] = product
            else:
                stage[m, 3] = product
            wide = product.astype(F32)

            def spread(g, inner):
                base = g * LONG
                here = pl.multiple_of(base + half * ROWS, ROWS)
                masked[c, pl.ds(here, ROWS), :] = jnp.where(lane_group == g, wide, 0.0).astype(BF16)

                @pl.when(half == 0)
                def _():
                    later = pl.multiple_of(base + ROWS, ROWS)
                    masked[c, pl.ds(later, ROWS), :] = jnp.zeros((ROWS, BLOCK), BF16)

                return inner

            lax.fori_loop(0, GROUPS, spread, 0)
            mine = pl.ds(pl.multiple_of(half * ROWS, ROWS), ROWS)
            past = pl.ds(pl.multiple_of(m * ROWS, ROWS), ROWS)
            convolved = pack[c, past, :] + dot(toeplitz[c, mine, :], masked[c])
            outgoing[m, :, c * BLOCK : (c + 1) * BLOCK] = (filtered[0] * convolved).astype(BF16)
        spread_out(outgoing.at[m], m)
        keep_copy(m).start()
        return carry

    lanes = lax.broadcasted_iota(jnp.int32, (ROWS, 128), 1)

    def pass_on(m):
        @pl.when(segment == 0)
        def _():
            @pl.when(m == 0)
            def _():
                def take(k, carry):
                    ids_from(k).wait_recv()
                    return carry

                lax.fori_loop(0, CHIPS, take, 0)
                embed_half.wait_recv()

            ids = ids_all[pl.ds(m * (ROWS // 16), ROWS // 16)].reshape(ROWS, 128)
            left = jnp.zeros((ROWS, BLOCK), F32)
            right = jnp.zeros((ROWS, BLOCK), F32)
            for v in range(4):
                hot = (ids == lanes + 128 * v).astype(F32).astype(BF16)
                left = left + dot(hot, embed_other[v * 128 : (v + 1) * 128, :])
                right = right + dot(hot, embed_ref[v * 128 : (v + 1) * 128, :])
            section_in[m, :, 0:BLOCK] = left.astype(BF16)
            section_in[m, :, BLOCK:WIDE] = right.astype(BF16)

        @pl.when(segment > 0)
        def _():
            hop_copy(m).wait_recv()

        spread_out(section_in.at[m], m)

    def put_out(m):
        @pl.when(m == 0)
        def _():
            w_out_local.wait()
            w_out_remote.wait_recv()

        acc[0:2] = jnp.zeros((2, ROWS, BLOCK), F32)

        def pair(i, inner):
            for p in range(2):
                j = arrived(m, order(2 * i + p))
                block = gathered[m, j]
                for c in range(2):
                    acc[c] += dot(block, w_out[c, rows_of(j), :])
            return inner

        lax.fori_loop(0, CHIPS // 2, pair, 0)
        for c in range(2):
            cols = slice(c * BLOCK, (c + 1) * BLOCK)
            outgoing[m, :, cols] = (section_in[m, :, cols].astype(F32) + acc[c]).astype(BF16)

        @pl.when(segment < 3)
        def _():
            hop_copy(m).start()

        half_copy(m).start()
        at = pl.ds(pl.multiple_of(m * ROWS, ROWS), ROWS)
        section_ref[at, :] = outgoing[m, :, BLOCK:WIDE]

    @pl.when(core == 0)
    def _():
        lax.fori_loop(0, CHUNKS, project, 0)
        write_cycles()
        for m in range(CHUNKS):
            half_copy(m).wait_recv()
            section_ref[m * ROWS : (m + 1) * ROWS, :] = section_half[m]
            keep_copy(m).wait_send()
        w_out_remote.wait_send()

    @pl.when(core == 1)
    def _():
        lead = jnp.where(segment == 0, 1, LEAD)

        def turn(i, carry):
            @pl.when(i < CHUNKS)
            def _():
                pass_on(i)

            m = i - lead

            @pl.when(m == CHUNKS - 1)
            def _():
                for n in range(CHUNKS):
                    keep_copy(n).wait_recv()
                write_cycles()

            @pl.when((m >= 0) & (m < CHUNKS))
            def _():
                put_out(m)

            return carry

        lax.fori_loop(0, CHUNKS + LEAD, turn, 0)
        for m in range(CHUNKS):
            half_copy(m).wait_send()

            @pl.when(segment < 3)
            def _():
                hop_copy(m).wait_send()

        def sent(k, carry):
            w_in_remote(k).wait_send()
            return carry

        lax.fori_loop(0, CHIPS, sent, 0)
        pack_copy.wait_send()
        toeplitz_copy.wait_send()

    def sent_chunk(i, carry):
        m, k = i // CHIPS, lax.rem(i, CHIPS)
        remote(
            section_in.at[0], gathered.at[m, chip], gather_send.at[m, k], gather_recv.at[m, k], sibling
        ).wait_send()
        return carry

    lax.fori_loop(0, CHUNKS * CHIPS, sent_chunk, 0)

    @pl.when((segment == 0) & (core == 1))
    def _():
        ids_pair.wait_send()

    @pl.when((segment == 0) & (core == 0))
    def _():
        def sent(k, carry):
            ids_to(k).wait_send()
            return carry

        lax.fori_loop(0, CHIPS, sent, 0)
        embed_half.wait_send()


def local(
    token_ids,
    cached_len,
    embed,
    gain,
    w_in,
    short_filter,
    long_filter,
    w_out,
    short_cycle,
    long_cycle,
):
    vmem = pl.BlockSpec(memory_space=pltpu.VMEM)
    smem = pl.BlockSpec(memory_space=pltpu.SMEM)
    anywhere = pl.BlockSpec(memory_space=pl.ANY)
    dma = pltpu.SemaphoreType.DMA
    section, new_short, new_long = pl.pallas_call(
        kernel,
        out_shape=(
            jax.ShapeDtypeStruct((CHUNKS * ROWS, BLOCK), BF16),
            jax.ShapeDtypeStruct((REQUESTS, 3, LONG, BLOCK), BF16),
            jax.ShapeDtypeStruct((REQUESTS, LONG, BLOCK), BF16),
        ),
        in_specs=[smem, smem, vmem, vmem, anywhere, vmem, vmem, anywhere, vmem, vmem],
        out_specs=(vmem, vmem, vmem),
        scratch_shapes=[
            pltpu.VMEM((2, 3, D, BLOCK), BF16),
            pltpu.VMEM((2, D, BLOCK), BF16),
            pltpu.VMEM((CHUNKS, CHIPS, ROWS, WIDE), BF16),
            pltpu.VMEM((CHUNKS, ROWS, WIDE), BF16),
            pltpu.VMEM((CHUNKS, ROWS, WIDE), BF16),
            pltpu.VMEM((6, ROWS, BLOCK), F32),
            pltpu.VMEM((ROWS, 128), F32),
            pltpu.VMEM((6, ROWS + 8, BLOCK), F32),
            pltpu.VMEM((2, GROUPS * LONG, BLOCK), BF16),
            pltpu.VMEM((2, LONG, GROUPS * LONG), BF16),
            pltpu.VMEM((LONG, GROUPS * LONG), BF16),
            pltpu.VMEM((2, PACK, BLOCK), F32),
            pltpu.VMEM((GROUPS, 2 * LONG), F32),
            pltpu.VMEM((CHUNKS, 4, ROWS, BLOCK), BF16),
            pltpu.VMEM((CHUNKS, 4, ROWS, BLOCK), BF16),
            pltpu.VMEM((CHIPS, 16, 128), jnp.int32),
            pltpu.VMEM((16, 128), jnp.int32),
            pltpu.VMEM((512, BLOCK), BF16),
            pltpu.VMEM((CHUNKS, ROWS, BLOCK), BF16),
            dma((CHUNKS, CHIPS)),
            dma((CHUNKS, CHIPS)),
            dma((CHUNKS,)),
            dma((CHUNKS,)),
            dma((CHIPS,)),
            dma((2, CHIPS)),
            dma,
            dma((2,)),
            dma((3,)),
            dma((3,)),
            dma((CHUNKS,)),
            dma((CHUNKS,)),
            dma((CHUNKS,)),
            dma((CHUNKS,)),
            dma((CHIPS + 1,)),
            dma((CHIPS + 1,)),
        ],
        compiler_params=pltpu.CompilerParams(
            collective_id=0, has_side_effects=True, vmem_limit_bytes=56 * 2**20
        ),
        name="layers",
    )(
        token_ids,
        cached_len,
        embed,
        gain,
        w_in[0].transpose(1, 0, 2),
        short_filter.reshape(SHORT * 3, 1, BLOCK),
        long_filter[0].T,
        w_out[0],
        short_cycle[0].transpose(0, 2, 1, 3),
        long_cycle[0],
    )
    return section[None], new_short.transpose(0, 2, 1, 3)[None], new_long[None]


def solution(mesh):
    in_specs = (
        P("seq"),
        P(),
        P(None, "seq"),
        P("segment", None),
        P("segment", None, None, "seq"),
        P("segment", None, None, "seq"),
        P("segment", None, "seq"),
        P("segment", None, "seq"),
        P("segment", None, None, None, "seq"),
        P("segment", None, None, "seq"),
    )
    out_specs = (
        P("segment", None, "seq"),
        P("segment", None, None, None, "seq"),
        P("segment", None, None, "seq"),
    )
    return jax.shard_map(local, mesh=mesh, in_specs=in_specs, out_specs=out_specs, check_vma=False)
```

time: 547 us -> 185 us (0.34); the launches traced: 538 us -> 185 us
  waiting for transfers between devices: 379 us -> 0 us
  Pallas kernels: 0 us -> 179 us
  matrix products: 64.9 us -> 0 us
  other arithmetic: 26.7 us -> 0 us
  between operations: 21.3 us -> 0.64 us
  local copies, waits for them, and re-layouts: 25.4 us -> 4.9 us
  blocking collectives: 14.9 us -> 0 us
    all_gather x8 -> x0, waiting for transfers between devices: 363 us -> none  [the longest x4 189 us: local(): shard_piece = lax.all_gather(mixed, 'seq', axis=1, tiled=True)]
    pallas_call x0 -> x1, Pallas kernels: none -> 179 us  [local(): pl.pallas_call(kernel, out_shape=(jax.ShapeDtypeStruct((CHUNKS * ROWS, BL...]
    dot_general x9 -> x0, matrix products: 53.5 us -> none  [the longest x4 33 us: local(): projected = jnp.dot(normed, proj_in, preferred_element_type=jnp.float32)]
    ppermute x3 -> x0, waiting for transfers between devices: 16.3 us -> none  [from_behind(): return lax.ppermute(block, axis, route)]
    unnamed x58 -> x3, local copies, waits for them, and re-layouts: 19.8 us -> 4.9 us
    unnamed x1 -> x0, blocking collectives: 14.9 us -> none
    reduce_sum x4 -> x0, other arithmetic: 13 us -> none  [local(): jnp.mean(widened * widened, axis=1, keepdims=True) + 1e-06]
    conv_general_dilated x8 -> x0, matrix products: 11.5 us -> none  [local(): lax.conv_general_dilated(carried[1:].astype(jnp.float32)[None], kernel, w...]
  transfers between devices with their start and end apart: 11 -> 0, of which waited for: 11 -> 0; matrix products, arithmetic and copies ran while one was open for 5% -> 0% of each run, Pallas kernels for 0% -> 0%
where the time goes in v1:
time: 185 us
  Pallas kernels  179 us (97%)
  local copies, waits for them, and re-layouts  4.9 us (3%)
    pallas_call x1, Pallas kernels, local(): pl.pallas_call(kernel, out_shape=(jax.ShapeDtypeStruct((CHUNKS * ROWS, BL...  179 us
    unnamed x3, local copies, waits for them, and re-layouts  4.9 us

profile of v1, /device:TPU:7, one launch (start us, length us, event | category | flops | bytes accessed | tf_op | source)
XLA Modules:
  0.0 184.7 jit_solution(5425684536045066558)
XLA Ops:
  0.6 179.2 %layers.1 = (bf16[256,256]{1,0:T(8,128)(2,1)}, bf16[2,3,128,256]{3,2,1,0:T(8,128)(2,1)}, bf16[2,128,256]{2,1,0:T(8,128)(2,1)}) custom-call(s32[8]{0:T(128)} %ids_ref.1, s32[2]{0:T(128)} %len_ref.1, bf16[512,256]{1,0:T(8,128)(2,1)} %embed_ref.1, f32[1,8192]{1,0:T(1,128)} %gain_ref.1, bf16[3,8192,256]{2,1,0:T(8,128)(2,1)} %bitcast.17, f32[21,1,256]{2,1,0:T(1,128)} %bitcast.24, ...), custom_call_target="tpu_custom_call" | custom-call | tf_op jit(solution)/shard_map/layers/pallas_call | solution.py:550
  179.8 1.6 copy.16
  181.4 1.8 copy.17
  183.1 1.6 copy.18

commit v2 on v1

--- a/solution.py
+++ b/solution.py
@@ -14,13 +14,12 @@
 ROWS = 64
 CHUNKS = 4
 BLOCK = 256
-WIDE = 2 * BLOCK
 GROUP = 16
 GROUPS = BLOCK // GROUP
 TAIL = REQUESTS * LONG
 TAPS = TAIL + REQUESTS * 3 * 8
 PACK = TAPS + 3 * 8
-LEAD = 2
+LEAD = 3
 MESH = pl.DeviceIdType.MESH
 F32 = jnp.float32
 BF16 = jnp.bfloat16
@@ -28,10 +27,6 @@
 
 def dot(a, b):
     return jnp.dot(a, b, preferred_element_type=F32)
-
-
-def folded(i):
-    return i + (i // 2) * (5 - 2 * i)
 
 
 def kernel(
@@ -67,8 +62,11 @@
     ids_own,
     embed_other,
     section_half,
-    gather_send,
-    gather_recv,
+    near_send,
+    next_send,
+    near_recv,
+    far_send,
+    far_recv,
     hop_send,
     hop_recv,
     w_in_send,
@@ -91,66 +89,92 @@
     row_z, row_y = chip // SIDE, lax.rem(chip, SIDE)
     sibling = (segment, chip * 2 + 1 - core)
 
-    def chip_at(k, sign):
-        dz, dy = folded(k // SIDE), folded(lax.rem(k, SIDE))
-        z = lax.rem(row_z + sign * dz + SIDE, SIDE)
-        y = lax.rem(row_y + sign * dy + SIDE, SIDE)
-        return z * SIDE + y
+    def along(c, step):
+        if c == 0:
+            return row_z * SIDE + lax.rem(row_y + step, SIDE)
+        return lax.rem(row_z + step, SIDE) * SIDE + row_y
+
+    places = (row_z, row_y)
 
     def remote(src, dst, send, recv, where):
         return pltpu.make_async_remote_copy(
             src_ref=src, dst_ref=dst, send_sem=send, recv_sem=recv, device_id=where, device_id_type=MESH
         )
 
-    def rows_of(j):
-        return pl.ds(pl.multiple_of(j * WIDE, WIDE), WIDE)
-
     barrier = pltpu.get_barrier_semaphore()
 
-    def greet(k, carry):
+    before = lax.rem(segment + 3, 4)
+    after = lax.rem(segment + 1, 4)
+
+    def greet(where, at, core_of):
         pl.semaphore_signal(
-            barrier, inc=1, device_id=(segment, k * 2 + 1 - core), device_id_type=MESH
+            barrier, inc=1, device_id=(where, at * 2 + core_of), device_id_type=MESH
         )
-        return carry
-
-    lax.fori_loop(0, CHIPS, greet, 0)
+
+    near = [along(c, step) for c in range(2) for step in range(1, SIDE)]
+    for at in near:
+        greet(segment, at, core)
+
+    @pl.when(core == 0)
+    def _():
+        for at in near + [chip]:
+            greet(segment, at, 1)
+            greet(before, at, 1)
 
     @pl.when(core == 1)
     def _():
-        for step in (1, 3):
-            pl.semaphore_signal(
-                barrier, inc=1, device_id=(lax.rem(segment + step, 4), seq), device_id_type=MESH
-            )
-
-    def w_in_local(k):
-        rows = rows_of(chip_at(k, 1))
+        def greet_one(k, carry):
+            greet(segment, k, 0)
+            return carry
+
+        lax.fori_loop(0, CHIPS, greet_one, 0)
+        greet(before, chip, 1)
+
+    def group(c, step):
+        return lax.rem(places[c] + step, SIDE)
+
+    def w_in_part(c, step):
+        i = group(c, step)
+        return w_in_ref.at[:, i, :, 0] if c == 0 else w_in_ref.at[:, :, i, 1]
+
+    def w_in_local(c, step):
         return pltpu.make_async_copy(
-            w_in_ref.at[:, rows, :], w_in.at[0, :, rows, :], w_in_recv.at[0, k]
+            w_in_part(c, step), w_in.at[0, c, group(c, step)], w_in_recv.at[0, c, step]
         )
 
-    def w_in_remote(k):
-        rows = rows_of(chip_at(k, 1))
+    def w_in_remote(c, step):
         return remote(
-            w_in_ref.at[:, rows, :], w_in.at[1, :, rows, :], w_in_send.at[k], w_in_recv.at[1, k], sibling
+            w_in_part(c, step),
+            w_in.at[1, c, group(c, step)],
+            w_in_send.at[c, step],
+            w_in_recv.at[1, c, step],
+            sibling,
         )
 
-    w_out_local = pltpu.make_async_copy(w_out_ref, w_out.at[1], w_out_recv.at[1])
-    w_out_remote = remote(w_out_ref, w_out.at[0], w_out_send, w_out_recv.at[0], sibling)
-
-    def order(i):
-        return lax.rem(i + 1, CHIPS)
+    STEPS = [(c, step) for step in (0, 1, 3, 2) for c in range(2)]
+
+    def w_out_part(c, i):
+        return w_out_ref.at[i, :, 0] if c == 0 else w_out_ref.at[:, i, 1]
+
+    PARTS = [(c, i) for c in range(2) for i in range(SIDE)]
+    w_out_local = [
+        pltpu.make_async_copy(w_out_part(c, i), w_out.at[1, c, i], w_out_recv.at[1, c, i])
+        for c, i in PARTS
+    ]
+    w_out_remote = [
+        remote(w_out_part(c, i), w_out.at[0, c, i], w_out_send.at[c, i], w_out_recv.at[0, c, i], sibling)
+        for c, i in PARTS
+    ]
 
     @pl.when(core == 0)
     def _():
-        def begin(i, carry):
-            w_in_local(order(i)).start()
-            return carry
-
-        lax.fori_loop(0, CHIPS, begin, 0)
+        for c, step in STEPS:
+            w_in_local(c, (SIDE - step) % SIDE).start()
 
     @pl.when(core == 1)
     def _():
-        w_out_local.start()
+        for copy in w_out_local:
+            copy.start()
 
     sub = lax.broadcasted_iota(jnp.int32, (8, 128), 0)
     mine = jnp.zeros((8, 128), jnp.int32)
@@ -167,11 +191,11 @@
 
     @pl.when(core == 0)
     def _():
-        pl.semaphore_wait(barrier, CHIPS)
+        pl.semaphore_wait(barrier, len(near) + CHIPS)
 
     @pl.when(core == 1)
     def _():
-        pl.semaphore_wait(barrier, CHIPS + 2)
+        pl.semaphore_wait(barrier, 3 * len(near) + 3)
 
     ids_pair = remote(
         ids_own.at[pl.ds(8, 8)], ids_own.at[pl.ds(8, 8)], ids_send.at[CHIPS], ids_recv.at[CHIPS], sibling
@@ -203,15 +227,13 @@
 
     @pl.when(core == 1)
     def _():
-        def begin(i, carry):
-            w_in_remote(order(i)).start()
-            return carry
-
-        lax.fori_loop(0, CHIPS, begin, 0)
+        for c, step in STEPS:
+            w_in_remote(c, (SIDE - step) % SIDE).start()
 
     @pl.when(core == 0)
     def _():
-        w_out_remote.start()
+        for copy in w_out_remote:
+            copy.start()
 
     flip_from = lax.broadcasted_iota(jnp.int32, (LONG, 2 * LONG), 0)
     flip_to = lax.broadcasted_iota(jnp.int32, (LONG, 2 * LONG), 1)
@@ -223,6 +245,7 @@
         return pl.ds(pl.multiple_of(g * LONG, LONG), LONG)
 
     def expand(g, carry):
+        masked[1, group_columns(g), :] = jnp.zeros((LONG, BLOCK), BF16)
         line = jnp.broadcast_to(reversed_taps[pl.ds(g, 1), :], (LONG, 2 * LONG))
         turned = pltpu.roll(line, 0, 1, stride=1, stride_axis=0)
         toeplitz_old[:, group_columns(g)] = turned[:, :LONG].astype(BF16)
@@ -265,30 +288,56 @@
         pack_copy.start()
         toeplitz_copy.start()
 
-    def spread_out(src, m):
-        def begin(i, carry):
-            k = order(i)
-            target = (segment, chip_at(k, -1) * 2 + 1 - core)
+    def near_copies(src, m, where, sems):
+        return [
             remote(
-                src, gathered.at[m, chip], gather_send.at[m, k], gather_recv.at[m, k], target
-            ).start()
-            return carry
-
-        lax.fori_loop(0, CHIPS, begin, 0)
-
-    def arrived(m, k):
-        j = chip_at(k, 1)
-        remote(
-            section_in.at[0], gathered.at[m, j], gather_send.at[m, k], gather_recv.at[m, k], sibling
-        ).wait_recv()
-        return j
+                src.at[m, c],
+                gathered.at[m, c, places[c], places[1 - c]],
+                sems.at[m, c, step],
+                near_recv.at[m, c, step],
+                (where, along(c, step) * 2 + 1 - core),
+            )
+            for step in (1, 3, 2, 0)
+            for c in range(2)
+        ]
+
+    def far_copy(m, c, step):
+        block = gathered.at[m, c, places[c]]
+        return remote(
+            block,
+            block,
+            far_send.at[m, c, step],
+            far_recv.at[m, c, step],
+            (segment, along(1 - c, step) * 2 + core),
+        )
+
+    def pass_along(m):
+        for c in range(2):
+            for step in range(SIDE):
+                remote(
+                    outgoing.at[0, 0],
+                    gathered.at[m, c, places[c], lax.rem(places[1 - c] + SIDE - step, SIDE)],
+                    next_send.at[m, c, step],
+                    near_recv.at[m, c, step],
+                    sibling,
+                ).wait_recv()
+            for step in (1, 3, 2):
+                far_copy(m, c, step).start()
+
+    def collect(m, use):
+        for c, step in STEPS:
+            i = lax.rem(places[c] + SIDE - step, SIDE)
+            if step:
+                block = gathered.at[m, c, i]
+                remote(block, block, far_send.at[m, c, step], far_recv.at[m, c, step], sibling).wait_recv()
+            use(c, i, (SIDE - step) % SIDE, jnp.concatenate([gathered[m, c, i, k] for k in range(SIDE)], axis=1))
 
     def keep_copy(m):
         return remote(stage.at[m], keep.at[m], keep_send.at[m], keep_recv.at[m], sibling)
 
     def half_copy(m):
         return remote(
-            outgoing.at[m, :, pl.ds(0, BLOCK)], section_half.at[m], half_send.at[m], half_recv.at[m], sibling
+            outgoing.at[m, 0], section_half.at[m], half_send.at[m], half_recv.at[m], sibling
         )
 
     def hop_copy(m):
@@ -297,7 +346,7 @@
             section_in.at[m],
             hop_send.at[m],
             hop_recv.at[m],
-            (lax.rem(segment + 1, 4), seq),
+            (after, seq),
         )
 
     def write_cycles():
@@ -316,28 +365,27 @@
         acc[...] = jnp.zeros_like(acc)
         squares[...] = jnp.zeros_like(squares)
 
-        def pair(i, inner):
-            for p in range(2):
-                k = order(2 * i + p)
-                j = arrived(m, k)
-
-                @pl.when(m == 0)
-                def _():
-                    w_in_local(k).wait()
-                    w_in_remote(k).wait_recv()
-
-                wide = gathered[m, j].astype(F32)
-                power = wide * wide
-                squares[...] += (
-                    power[:, 0:128] + power[:, 128:256] + power[:, 256:384] + power[:, 384:512]
-                )
-                scaled = (wide * gain_ref[:, rows_of(j)]).astype(BF16)
-                for c in range(2):
-                    for b in range(3):
-                        acc[c * 3 + b] += dot(scaled, w_in[c, b, rows_of(j), :])
-            return inner
-
-        lax.fori_loop(0, CHIPS // 2, pair, 0)
+        def use(c, i, step, block):
+            @pl.when(m == 0)
+            def _():
+                w_in_local(c, step).wait()
+                w_in_remote(c, step).wait_recv()
+
+            wide = block.astype(F32)
+            power = wide * wide
+            total = power[:, 0:128]
+            for v in range(1, SIDE * 2):
+                total = total + power[:, v * 128 : (v + 1) * 128]
+            squares[...] += total
+            gains = jnp.concatenate([gain_ref[i, k, 0] if c == 0 else gain_ref[k, i, 1] for k in range(SIDE)], axis=1)
+            scaled = (wide * gains).astype(BF16)
+            for n in range(2):
+                for b in range(3):
+                    weights = w_in[n, c, i, b].reshape(SIDE * BLOCK, BLOCK)
+                    acc[n * 3 + b] += dot(scaled, weights)
+
+        pass_along(m)
+        collect(m, use)
         scale = lax.rsqrt(jnp.sum(squares[...], axis=1, keepdims=True) * (1.0 / D) + 1e-6)
         half = lax.rem(m, 2)
         request = m // 2
@@ -383,81 +431,77 @@
                 base = g * LONG
                 here = pl.multiple_of(base + half * ROWS, ROWS)
                 masked[c, pl.ds(here, ROWS), :] = jnp.where(lane_group == g, wide, 0.0).astype(BF16)
-
-                @pl.when(half == 0)
-                def _():
-                    later = pl.multiple_of(base + ROWS, ROWS)
-                    masked[c, pl.ds(later, ROWS), :] = jnp.zeros((ROWS, BLOCK), BF16)
-
                 return inner
 
-            lax.fori_loop(0, GROUPS, spread, 0)
+            lax.fori_loop(0, GROUPS, spread, 0, unroll=4)
             mine = pl.ds(pl.multiple_of(half * ROWS, ROWS), ROWS)
             past = pl.ds(pl.multiple_of(m * ROWS, ROWS), ROWS)
             convolved = pack[c, past, :] + dot(toeplitz[c, mine, :], masked[c])
-            outgoing[m, :, c * BLOCK : (c + 1) * BLOCK] = (filtered[0] * convolved).astype(BF16)
-        spread_out(outgoing.at[m], m)
+            outgoing[m, c] = (filtered[0] * convolved).astype(BF16)
+        for copy in near_copies(outgoing, m, segment, near_send):
+            copy.start()
         keep_copy(m).start()
+
         return carry
 
     lanes = lax.broadcasted_iota(jnp.int32, (ROWS, 128), 1)
 
     def pass_on(m):
-        @pl.when(segment == 0)
+        @pl.when(m == 0)
         def _():
-            @pl.when(m == 0)
-            def _():
-                def take(k, carry):
-                    ids_from(k).wait_recv()
-                    return carry
-
-                lax.fori_loop(0, CHIPS, take, 0)
-                embed_half.wait_recv()
-
-            ids = ids_all[pl.ds(m * (ROWS // 16), ROWS // 16)].reshape(ROWS, 128)
-            left = jnp.zeros((ROWS, BLOCK), F32)
-            right = jnp.zeros((ROWS, BLOCK), F32)
-            for v in range(4):
-                hot = (ids == lanes + 128 * v).astype(F32).astype(BF16)
-                left = left + dot(hot, embed_other[v * 128 : (v + 1) * 128, :])
-                right = right + dot(hot, embed_ref[v * 128 : (v + 1) * 128, :])
-            section_in[m, :, 0:BLOCK] = left.astype(BF16)
-            section_in[m, :, BLOCK:WIDE] = right.astype(BF16)
+            def take(k, carry):
+                ids_from(k).wait_recv()
+                return carry
+
+            lax.fori_loop(0, CHIPS, take, 0)
+            embed_half.wait_recv()
+
+        ids = ids_all[pl.ds(m * (ROWS // 16), ROWS // 16)].reshape(ROWS, 128)
+        left = jnp.zeros((ROWS, BLOCK), F32)
+        right = jnp.zeros((ROWS, BLOCK), F32)
+        for v in range(4):
+            hot = (ids == lanes + 128 * v).astype(F32).astype(BF16)
+            left = left + dot(hot, embed_other[v * 128 : (v + 1) * 128, :])
+            right = right + dot(hot, embed_ref[v * 128 : (v + 1) * 128, :])
+        section_in[m, 0] = left.astype(BF16)
+        section_in[m, 1] = right.astype(BF16)
+
+        for copy in near_copies(section_in, m, segment, near_send):
+            copy.start()
+
+    def put_out(m):
+        @pl.when(m == 0)
+        def _():
+            for copy in w_out_local:
+                copy.wait()
+            for copy in w_out_remote:
+                copy.wait_recv()
+
+        acc[0:2] = jnp.zeros((2, ROWS, BLOCK), F32)
+
+        def use(c, i, step, block):
+            for n in range(2):
+                acc[n] += dot(block, w_out[n, c, i].reshape(SIDE * BLOCK, BLOCK))
+
+        pass_along(m)
+        collect(m, use)
 
         @pl.when(segment > 0)
         def _():
             hop_copy(m).wait_recv()
 
-        spread_out(section_in.at[m], m)
-
-    def put_out(m):
-        @pl.when(m == 0)
-        def _():
-            w_out_local.wait()
-            w_out_remote.wait_recv()
-
-        acc[0:2] = jnp.zeros((2, ROWS, BLOCK), F32)
-
-        def pair(i, inner):
-            for p in range(2):
-                j = arrived(m, order(2 * i + p))
-                block = gathered[m, j]
-                for c in range(2):
-                    acc[c] += dot(block, w_out[c, rows_of(j), :])
-            return inner
-
-        lax.fori_loop(0, CHIPS // 2, pair, 0)
         for c in range(2):
-            cols = slice(c * BLOCK, (c + 1) * BLOCK)
-            outgoing[m, :, cols] = (section_in[m, :, cols].astype(F32) + acc[c]).astype(BF16)
+            outgoing[m, c] = (section_in[m, c].astype(F32) + acc[c]).astype(BF16)
 
         @pl.when(segment < 3)
         def _():
+            for copy in near_copies(outgoing, m, after, next_send):
+                copy.start()
             hop_copy(m).start()
 
         half_copy(m).start()
         at = pl.ds(pl.multiple_of(m * ROWS, ROWS), ROWS)
-        section_ref[at, :] = outgoing[m, :, BLOCK:WIDE]
+        section_ref[at, :] = outgoing[m, 1]
 
     @pl.when(core == 0)
     def _():
@@ -467,14 +511,15 @@
             half_copy(m).wait_recv()
             section_ref[m * ROWS : (m + 1) * ROWS, :] = section_half[m]
             keep_copy(m).wait_send()
-        w_out_remote.wait_send()
+        for copy in w_out_remote:
+            copy.wait_send()
 
     @pl.when(core == 1)
     def _():
-        lead = jnp.where(segment == 0, 1, LEAD)
+        lead = jnp.where(segment == 0, LEAD, 0)
 
         def turn(i, carry):
-            @pl.when(i < CHUNKS)
+            @pl.when((segment == 0) & (i < CHUNKS))
             def _():
                 pass_on(i)
 
@@ -500,22 +545,34 @@
             def _():
                 hop_copy(m).wait_send()
 
-        def sent(k, carry):
-            w_in_remote(k).wait_send()
-            return carry
-
-        lax.fori_loop(0, CHIPS, sent, 0)
+        for c, step in STEPS:
+            w_in_remote(c, step).wait_send()
         pack_copy.wait_send()
         toeplitz_copy.wait_send()
 
-    def sent_chunk(i, carry):
-        m, k = i // CHIPS, lax.rem(i, CHIPS)
-        remote(
-            section_in.at[0], gathered.at[m, chip], gather_send.at[m, k], gather_recv.at[m, k], sibling
-        ).wait_send()
+    def all_sent(where, sems):
+        def sent(m, carry):
+            for copy in near_copies(outgoing, m, where, sems):
+                copy.wait_send()
+            return carry
+
+        lax.fori_loop(0, CHUNKS, sent, 0)
+
+    @pl.when((core == 0) | (segment == 0))
+    def _():
+        all_sent(segment, near_send)
+
+    @pl.when((core == 1) & (segment < 3))
+    def _():
+        all_sent(after, next_send)
+
+    def far_sent(m, carry):
+        for c in range(2):
+            for step in (1, 3, 2):
+                far_copy(m, c, step).wait_send()
         return carry
 
-    lax.fori_loop(0, CHUNKS * CHIPS, sent_chunk, 0)
+    lax.fori_loop(0, CHUNKS, far_sent, 0)
 
     @pl.when((segment == 0) & (core == 1))
     def _():
@@ -529,6 +586,11 @@
 
         lax.fori_loop(0, CHIPS, sent, 0)
         embed_half.wait_send()
+
+
+def write_out(*refs):
+    for i in range(3):
+        refs[3 + i][...] = refs[i][...]
 
 
 def local(
@@ -557,11 +619,11 @@
         in_specs=[smem, smem, vmem, vmem, anywhere, vmem, vmem, anywhere, vmem, vmem],
         out_specs=(vmem, vmem, vmem),
         scratch_shapes=[
-            pltpu.VMEM((2, 3, D, BLOCK), BF16),
-            pltpu.VMEM((2, D, BLOCK), BF16),
-            pltpu.VMEM((CHUNKS, CHIPS, ROWS, WIDE), BF16),
-            pltpu.VMEM((CHUNKS, ROWS, WIDE), BF16),
-            pltpu.VMEM((CHUNKS, ROWS, WIDE), BF16),
+            pltpu.VMEM((2, 2, SIDE, 3, SIDE, BLOCK, BLOCK), BF16),
+            pltpu.VMEM((2, 2, SIDE, SIDE, BLOCK, BLOCK), BF16),
+            pltpu.VMEM((CHUNKS, 2, SIDE, SIDE, ROWS, BLOCK), BF16),
+            pltpu.VMEM((CHUNKS, 2, ROWS, BLOCK), BF16),
+            pltpu.VMEM((CHUNKS, 2, ROWS, BLOCK), BF16),
             pltpu.VMEM((6, ROWS, BLOCK), F32),
             pltpu.VMEM((ROWS, 128), F32),
             pltpu.VMEM((6, ROWS + 8, BLOCK), F32),
@@ -576,14 +638,17 @@
             pltpu.VMEM((16, 128), jnp.int32),
             pltpu.VMEM((512, BLOCK), BF16),
             pltpu.VMEM((CHUNKS, ROWS, BLOCK), BF16),
-            dma((CHUNKS, CHIPS)),
-            dma((CHUNKS, CHIPS)),
+            dma((CHUNKS, 2, SIDE)),
+            dma((CHUNKS, 2, SIDE)),
+            dma((CHUNKS, 2, SIDE)),
+            dma((CHUNKS, 2, SIDE)),
+            dma((CHUNKS, 2, SIDE)),
             dma((CHUNKS,)),
             dma((CHUNKS,)),
-            dma((CHIPS,)),
-            dma((2, CHIPS)),
-            dma,
-            dma((2,)),
+            dma((2, SIDE)),
+            dma((2, 2, SIDE)),
+            dma((2, SIDE)),
+            dma((2, 2, SIDE)),
             dma((3,)),
             dma((3,)),
             dma((CHUNKS,)),
@@ -601,14 +666,21 @@
         token_ids,
         cached_len,
         embed,
-        gain,
-        w_in[0].transpose(1, 0, 2),
+        gain.reshape(SIDE, SIDE, 2, 1, BLOCK),
+        w_in[0].transpose(1, 0, 2).reshape(3, SIDE, SIDE, 2, BLOCK, BLOCK),
         short_filter.reshape(SHORT * 3, 1, BLOCK),
         long_filter[0].T,
-        w_out[0],
+        w_out[0].reshape(SIDE, SIDE, 2, BLOCK, BLOCK),
         short_cycle[0].transpose(0, 2, 1, 3),
         long_cycle[0],
     )
+    section, new_short, new_long = pl.pallas_call(
+        write_out,
+        out_shape=tuple(jax.ShapeDtypeStruct(x.shape, x.dtype) for x in (section, new_short, new_long)),
+        in_specs=[vmem] * 3,
+        out_specs=(vmem,) * 3,
+        name="write_out",
+    )(section, new_short, new_long)
     return section[None], new_short.transpose(0, 2, 1, 3)[None], new_long[None]
 
 

time: 185 us -> 162 us (0.88)
  Pallas kernels: 179 us -> 161 us
  local copies, waits for them, and re-layouts: 4.9 us -> 0 us
    pallas_call x1, Pallas kernels: 179 us -> 159 us  [local(): pl.pallas_call(kernel, out_shape=(jax.ShapeDtypeStruct((CHUNKS * ROWS, BL...]
    unnamed x3 -> x0, local copies, waits for them, and re-layouts: 4.9 us -> none
    pallas_call x0 -> x1, Pallas kernels: none -> 1.94 us  [local(): pl.pallas_call(write_out, out_shape=tuple((jax.ShapeDtypeStruct(x.shape,...]
where the time goes in v2:
time: 162 us
  Pallas kernels  161 us (99%)
    pallas_call x1, Pallas kernels, local(): pl.pallas_call(kernel, out_shape=(jax.ShapeDtypeStruct((CHUNKS * ROWS, BL...  159 us

profile of v2, /device:TPU:7, one launch (start us, length us, event | category | flops | bytes accessed | tf_op | source)
XLA Modules:
  0.0 161.6 jit_solution(17851544626177533332)
XLA Ops:
  0.6 159.0 %layers.1 = (bf16[256,256]{1,0:T(8,128)(2,1)}, bf16[2,3,128,256]{3,2,1,0:T(8,128)(2,1)}, bf16[2,128,256]{2,1,0:T(8,128)(2,1)}) custom-call(s32[8]{0:T(128)} %ids_ref.1, s32[2]{0:T(128)} %len_ref.1, bf16[512,256]{1,0:T(8,128)(2,1)} %embed_ref.1, f32[4,4,2,1,256]{4,3,2,1,0:T(1,128)} %bitcast.24, bf16[3,4,4,2,256,256]{5,4,3,2,1,0:T(8,128)(2,1)} %bitcast.20, ...), custom_call_target="tpu_custom_call" | custom-call | tf_op jit(solution)/shard_map/layers/pallas_call | solution.py:612
  159.6 1.9 %write_out.1 = (bf16[256,256]{1,0:T(8,128)(2,1)}, bf16[2,3,128,256]{3,2,1,0:T(8,128)(2,1)}, bf16[2,128,256]{2,1,0:T(8,128)(2,1)}) custom-call(bf16[256,256]{1,0:T(8,128)(2,1)} %get-tuple-element.9.refs_0_, bf16[2,3,128,256]{3,2,1,0:T(8,128)(2,1)} %get-tuple-element.10.refs_1_, bf16[2,128,256]{2,1,0:T(8,128)(2,1)} %get-tuple-element.11.refs_2_), custom_call_target="tpu_custom_call" | custom-call | tf_op jit(solution)/shard_map/write_out/pallas_call | solution.py:677

commit v3 on v2

--- a/solution.py
+++ b/solution.py
@@ -19,7 +19,8 @@
 TAIL = REQUESTS * LONG
 TAPS = TAIL + REQUESTS * 3 * 8
 PACK = TAPS + 3 * 8
-LEAD = 3
+EARLY = 4
+LEAD = 2
 MESH = pl.DeviceIdType.MESH
 F32 = jnp.float32
 BF16 = jnp.bfloat16
@@ -52,6 +53,7 @@
     squares,
     extended,
     masked,
+    group_mask,
     toeplitz,
     toeplitz_old,
     pack,
@@ -151,7 +153,7 @@
             sibling,
         )
 
-    STEPS = [(c, step) for step in (0, 1, 3, 2) for c in range(2)]
+    STEPS = [(c, step) for step in (0, 2, 1, 3) for c in range(2)]
 
     def w_out_part(c, i):
         return w_out_ref.at[i, :, 0] if c == 0 else w_out_ref.at[:, i, 1]
@@ -227,8 +229,16 @@
 
     @pl.when(core == 1)
     def _():
-        for c, step in STEPS:
+        for c, step in STEPS[:EARLY]:
             w_in_remote(c, (SIDE - step) % SIDE).start()
+
+    def later_weights():
+        for c, step in STEPS[EARLY:]:
+            w_in_remote(c, (SIDE - step) % SIDE).start()
+
+    @pl.when((core == 1) & (segment > 0))
+    def _():
+        later_weights()
 
     @pl.when(core == 0)
     def _():
@@ -245,6 +255,7 @@
         return pl.ds(pl.multiple_of(g * LONG, LONG), LONG)
 
     def expand(g, carry):
+        group_mask[g] = jnp.broadcast_to((lane_group == g).astype(F32), (ROWS, BLOCK)).astype(BF16)
         masked[1, group_columns(g), :] = jnp.zeros((LONG, BLOCK), BF16)
         line = jnp.broadcast_to(reversed_taps[pl.ds(g, 1), :], (LONG, 2 * LONG))
         turned = pltpu.roll(line, 0, 1, stride=1, stride_axis=0)
@@ -288,7 +299,7 @@
         pack_copy.start()
         toeplitz_copy.start()
 
-    def near_copies(src, m, where, sems):
+    def near_copies(src, m, where, sems, halves=(0, 1)):
         return [
             remote(
                 src.at[m, c],
@@ -297,8 +308,8 @@
                 near_recv.at[m, c, step],
                 (where, along(c, step) * 2 + 1 - core),
             )
-            for step in (1, 3, 2, 0)
-            for c in range(2)
+            for step in (2, 1, 3, 0)
+            for c in halves
         ]
 
     def far_copy(m, c, step):
@@ -321,7 +332,7 @@
                     near_recv.at[m, c, step],
                     sibling,
                 ).wait_recv()
-            for step in (1, 3, 2):
+            for step in (2, 1, 3):
                 far_copy(m, c, step).start()
 
     def collect(m, use):
@@ -385,8 +396,6 @@
                     acc[n * 3 + b] += dot(scaled, weights)
 
         pass_along(m)
-        collect(m, use)
-        scale = lax.rsqrt(jnp.sum(squares[...], axis=1, keepdims=True) * (1.0 / D) + 1e-6)
         half = lax.rem(m, 2)
         request = m // 2
 
@@ -395,53 +404,46 @@
             pack_copy.wait_recv()
             toeplitz_copy.wait_recv()
 
+        @pl.when(half == 0)
+        def _():
+            for c in range(2):
+                for b in range(3):
+                    at = pl.multiple_of(TAIL + (request * 3 + b) * 8, 8)
+                    extended[c * 3 + b, 0:8, :] = pack[c, pl.ds(at, 8), :]
+
+        @pl.when(half == 1)
+        def _():
+            for e in range(6):
+                extended[e, 0:8, :] = extended[e, ROWS : ROWS + 8, :]
+
+        collect(m, use)
+        scale = lax.rsqrt(jnp.sum(squares[...], axis=1, keepdims=True) * (1.0 / D) + 1e-6)
+        mine = pl.ds(pl.multiple_of(half * ROWS, ROWS), ROWS)
+        past = pl.ds(pl.multiple_of(m * ROWS, ROWS), ROWS)
+
+        def filter_branch(c, b):
+            e = c * 3 + b
+            own = (acc[e] * scale).astype(BF16)
+            (keep if c == 0 else stage)[m, b] = own
+            extended[e, 8 : 8 + ROWS, :] = own.astype(F32)
+            total = None
+            for j in range(SHORT):
+                at = TAPS + b * 8 + j
+                term = pack[c, at : at + 1, :] * extended[e, 8 - j : 8 - j + ROWS, :]
+                total = term if total is None else total + term
+            return total
+
         for c in range(2):
-            filtered = []
-            for b in range(3):
-                e = c * 3 + b
-                own = (acc[e] * scale).astype(BF16)
-                if c == 0:
-                    keep[m, b] = own
-                else:
-                    stage[m, b] = own
-
-                @pl.when(half == 0)
-                def _():
-                    at = pl.multiple_of(TAIL + (request * 3 + b) * 8, 8)
-                    extended[e, 0:8, :] = pack[c, pl.ds(at, 8), :]
-
-                @pl.when(half == 1)
-                def _():
-                    extended[e, 0:8, :] = extended[e, ROWS : ROWS + 8, :]
-
-                extended[e, 8 : 8 + ROWS, :] = own.astype(F32)
-                total = jnp.zeros((ROWS, BLOCK), F32)
-                for j in range(SHORT):
-                    at = TAPS + b * 8 + j
-                    total = total + pack[c, at : at + 1, :] * extended[e, 8 - j : 8 - j + ROWS, :]
-                filtered.append(total)
-            product = (filtered[1] * filtered[2]).astype(BF16)
-            if c == 0:
-                keep[m, 3] = product
-            else:
-                stage[m, 3] = product
-            wide = product.astype(F32)
-
-            def spread(g, inner):
-                base = g * LONG
-                here = pl.multiple_of(base + half * ROWS, ROWS)
-                masked[c, pl.ds(here, ROWS), :] = jnp.where(lane_group == g, wide, 0.0).astype(BF16)
-                return inner
-
-            lax.fori_loop(0, GROUPS, spread, 0, unroll=4)
-            mine = pl.ds(pl.multiple_of(half * ROWS, ROWS), ROWS)
-            past = pl.ds(pl.multiple_of(m * ROWS, ROWS), ROWS)
+            product = (filter_branch(c, 1) * filter_branch(c, 2)).astype(BF16)
+            (keep if c == 0 else stage)[m, 3] = product
+            for g in range(GROUPS):
+                here = pl.multiple_of(g * LONG + half * ROWS, ROWS)
+                masked[c, pl.ds(here, ROWS), :] = product * group_mask[g]
             convolved = pack[c, past, :] + dot(toeplitz[c, mine, :], masked[c])
-            outgoing[m, c] = (filtered[0] * convolved).astype(BF16)
+            outgoing[m, c] = (filter_branch(c, 0) * convolved).astype(BF16)
         for copy in near_copies(outgoing, m, segment, near_send):
             copy.start()
         keep_copy(m).start()
-
         return carry
 
     lanes = lax.broadcasted_iota(jnp.int32, (ROWS, 128), 1)
@@ -484,6 +486,13 @@
                 acc[n] += dot(block, w_out[n, c, i].reshape(SIDE * BLOCK, BLOCK))
 
         pass_along(m)
+
+        @pl.when(m == CHUNKS - 1)
+        def _():
+            for n in range(CHUNKS):
+                keep_copy(n).wait_recv()
+            write_cycles()
+
         collect(m, use)
 
         @pl.when(segment > 0)
@@ -523,13 +532,11 @@
             def _():
                 pass_on(i)
 
+            @pl.when((segment == 0) & (i == 0))
+            def _():
+                later_weights()
+
             m = i - lead
-
-            @pl.when(m == CHUNKS - 1)
-            def _():
-                for n in range(CHUNKS):
-                    keep_copy(n).wait_recv()
-                write_cycles()
 
             @pl.when((m >= 0) & (m < CHUNKS))
             def _():
@@ -628,6 +635,7 @@
             pltpu.VMEM((ROWS, 128), F32),
             pltpu.VMEM((6, ROWS + 8, BLOCK), F32),
             pltpu.VMEM((2, GROUPS * LONG, BLOCK), BF16),
+            pltpu.VMEM((GROUPS, ROWS, BLOCK), BF16),
             pltpu.VMEM((2, LONG, GROUPS * LONG), BF16),
             pltpu.VMEM((LONG, GROUPS * LONG), BF16),
             pltpu.VMEM((2, PACK, BLOCK), F32),

time: 162 us -> 157 us (0.969)
  Pallas kernels: 161 us -> 156 us
    pallas_call x1, Pallas kernels: 159 us -> 154 us  [local(): pl.pallas_call(kernel, out_shape=(jax.ShapeDtypeStruct((CHUNKS * ROWS, BL...]
where the time goes in v3:
time: 157 us
  Pallas kernels  156 us (99%)
    pallas_call x1, Pallas kernels, local(): pl.pallas_call(kernel, out_shape=(jax.ShapeDtypeStruct((CHUNKS * ROWS, BL...  154 us

profile of v3, /device:TPU:7, one launch (start us, length us, event | category | flops | bytes accessed | tf_op | source)
XLA Modules:
  0.0 156.7 jit_solution(13592086061755631882)
XLA Ops:
  0.6 154.1 %layers.1 = (bf16[256,256]{1,0:T(8,128)(2,1)}, bf16[2,3,128,256]{3,2,1,0:T(8,128)(2,1)}, bf16[2,128,256]{2,1,0:T(8,128)(2,1)}) custom-call(s32[8]{0:T(128)} %ids_ref.1, s32[2]{0:T(128)} %len_ref.1, bf16[512,256]{1,0:T(8,128)(2,1)} %embed_ref.1, f32[4,4,2,1,256]{4,3,2,1,0:T(1,128)} %bitcast.24, bf16[3,4,4,2,256,256]{5,4,3,2,1,0:T(8,128)(2,1)} %bitcast.20, ...), custom_call_target="tpu_custom_call" | custom-call | tf_op jit(solution)/shard_map/layers/pallas_call | solution.py:619
  154.8 1.9 %write_out.1 = (bf16[256,256]{1,0:T(8,128)(2,1)}, bf16[2,3,128,256]{3,2,1,0:T(8,128)(2,1)}, bf16[2,128,256]{2,1,0:T(8,128)(2,1)}) custom-call(bf16[256,256]{1,0:T(8,128)(2,1)} %get-tuple-element.9.refs_0_, bf16[2,3,128,256]{3,2,1,0:T(8,128)(2,1)} %get-tuple-element.10.refs_1_, bf16[2,128,256]{2,1,0:T(8,128)(2,1)} %get-tuple-element.11.refs_2_), custom_call_target="tpu_custom_call" | custom-call | tf_op jit(solution)/shard_map/write_out/pallas_call | solution.py:685

commit v4 on v3

--- a/solution.py
+++ b/solution.py
@@ -619,9 +619,9 @@
     section, new_short, new_long = pl.pallas_call(
         kernel,
         out_shape=(
-            jax.ShapeDtypeStruct((CHUNKS * ROWS, BLOCK), BF16),
-            jax.ShapeDtypeStruct((REQUESTS, 3, LONG, BLOCK), BF16),
-            jax.ShapeDtypeStruct((REQUESTS, LONG, BLOCK), BF16),
+            pltpu.VMEM((CHUNKS * ROWS, BLOCK), BF16),
+            pltpu.VMEM((REQUESTS, 3, LONG, BLOCK), BF16),
+            pltpu.VMEM((REQUESTS, LONG, BLOCK), BF16),
         ),
         in_specs=[smem, smem, vmem, vmem, anywhere, vmem, vmem, anywhere, vmem, vmem],
         out_specs=(vmem, vmem, vmem),

time: 157 us -> 159 us (1.013)
  local copies, waits for them, and re-layouts: 0 us -> 2.05 us
    unnamed x0 -> x6, local copies, waits for them, and re-layouts: none -> 2.05 us
where the time goes in v4:
time: 159 us
  Pallas kernels  156 us (98%)
  local copies, waits for them, and re-layouts  2.05 us (1%)
    pallas_call x1, Pallas kernels, local(): pl.pallas_call(kernel, out_shape=(pltpu.VMEM((CHUNKS * ROWS, BLOCK), BF16...  154 us

profile of v4, /device:TPU:7, one launch (start us, length us, event | category | flops | bytes accessed | tf_op | source)
XLA Modules:
  0.0 158.7 jit_solution(3585339757486590880)
XLA Ops:
  0.6 154.1 %layers.1 = (bf16[256,256]{1,0:T(8,128)(2,1)S(1)}, bf16[2,3,128,256]{3,2,1,0:T(8,128)(2,1)S(1)}, bf16[2,128,256]{2,1,0:T(8,128)(2,1)S(1)}) custom-call(s32[8]{0:T(128)} %ids_ref.1, s32[2]{0:T(128)} %len_ref.1, bf16[512,256]{1,0:T(8,128)(2,1)} %embed_ref.1, f32[4,4,2,1,256]{4,3,2,1,0:T(1,128)} %bitcast.24, bf16[3,4,4,2,256,256]{5,4,3,2,1,0:T(8,128)(2,1)} %bitcast.20, ...), custom_call_target="tpu_custom_call" | custom-call | tf_op jit(solution)/shard_map/layers/pallas_call | solution.py:619
  154.7 0.0 copy-start
  154.7 0.7 copy-done
  155.5 0.0 copy-start.1
  155.5 0.7 copy-done.1
  156.1 0.0 copy-start.2
  156.1 0.6 copy-done.2
  156.8 1.9 %write_out.1 = (bf16[256,256]{1,0:T(8,128)(2,1)}, bf16[2,3,128,256]{3,2,1,0:T(8,128)(2,1)}, bf16[2,128,256]{2,1,0:T(8,128)(2,1)}) custom-call(bf16[256,256]{1,0:T(8,128)(2,1)} %copy-done.1, bf16[2,3,128,256]{3,2,1,0:T(8,128)(2,1)} %copy-done, bf16[2,128,256]{2,1,0:T(8,128)(2,1)} %copy-done.2), custom_call_target="tpu_custom_call" | custom-call | tf_op jit(solution)/shard_map/write_out/pallas_call | solution.py:685
Async XLA Ops:
  154.7 0.7 copy-start
  155.5 0.7 copy-start.1
  156.1 0.6 copy-start.2
